TPU v7x, 128 devices: a whole 4x4x4 slice. The times are simulated.
128 devices in a mesh: group: 16 (over z, y), local: 8 (over x, core).
Axes of the slice: x: 4, y: 4, z: 4, core: 2. Of those that a mesh axis runs over, the one named last changes fastest.
Arguments:
- tokens: bfloat16 [16384, 3584], P(('group', 'local')), may hold values from -6 to 6
- expert_ids: int32 [16384, 8], P(('group', 'local')), may hold values from 0 to 127, all different within a row; in each aligned block of 128 rows (0 to 127, 128 to 255, ...) at most 10 rows name the same one
- gate_weights: float32 [16384, 8], P(('group', 'local')), may hold values from 0.05 to 0.5
- w_gate: bfloat16 [128, 3584, 1024], P(('group', 'local')), may hold values from -0.09375 to 0.09375
- w_up: bfloat16 [128, 3584, 1024], P(('group', 'local')), may hold values from -0.09375 to 0.09375
- w_down: bfloat16 [128, 1024, 3584], P(('group', 'local')), may hold values from -0.1875 to 0.1875
Outputs:
- combined: bfloat16 [16384, 3584], P(('group', 'local'))
Inputs may be any that keep to these rules, and one draw needn't show every extreme that they name: `expert_ids`: within the rows of one device (aligned blocks of 128 rows) no expert is named by more than 10 rows, and in every draw some expert is named by exactly 10 rows of some device; each row names 8 different experts, and expert e is held by device e of group+local.
All inputs are finite; a program needn't handle non-finite values.
Results may differ from a plain program's by a relative error of at most 0.011.
Values may be sent and summed in bfloat16 or wider, within the bound.
A program may use at most 192 MiB of HBM per device.

v0:
```python
import jax
import jax.numpy as jnp
from jax import lax
from jax.sharding import PartitionSpec as P

CAP = 10


def body(tokens, expert_ids, gate_weights, w_gate, w_up, w_down):
    rows, width = tokens.shape
    experts = lax.axis_size("group") * lax.axis_size("local")
    quarter = width // 4
    labels = jnp.arange(experts, dtype=jnp.int32)
    hit = expert_ids[:, :, None] == labels[None, None, :]
    named = jnp.any(hit, axis=1)
    weight_te = jnp.sum(jnp.where(hit, gate_weights[:, :, None], 0.0), axis=1)
    below = (jnp.arange(rows)[:, None] > jnp.arange(rows)[None, :]).astype(jnp.bfloat16)
    place = jnp.dot(below, named.astype(jnp.bfloat16), preferred_element_type=jnp.float32).astype(jnp.int32)
    place = jnp.where(named, place, -1)
    pick = place.T[:, None, :] == jnp.arange(CAP, dtype=jnp.int32)[None, :, None]
    pick_bf = pick.reshape(experts * CAP, rows).astype(jnp.bfloat16)
    parts = [
        jnp.dot(pick_bf, tokens[:, q * quarter:(q + 1) * quarter], preferred_element_type=jnp.bfloat16)
        .reshape(experts, CAP, quarter)
        for q in range(4)
    ]
    arrived = lax.all_to_all(jnp.concatenate(parts, axis=1), ("group", "local"), split_axis=0, concat_axis=0, tiled=True)
    flat = jnp.concatenate(
        [arrived[:, q * CAP:(q + 1) * CAP].reshape(experts * CAP, quarter) for q in range(4)], axis=1
    )
    gate_part = jnp.dot(flat, w_gate[0], preferred_element_type=jnp.float32)
    lin_part = jnp.dot(flat, w_up[0], preferred_element_type=jnp.float32)
    hidden = (jax.nn.silu(gate_part) * lin_part).astype(jnp.bfloat16)
    results = jnp.concatenate(
        [
            jnp.dot(hidden, w_down[0][:, q * quarter:(q + 1) * quarter], preferred_element_type=jnp.float32)
            .astype(jnp.bfloat16)
            .reshape(experts, CAP, quarter)
            for q in range(4)
        ],
        axis=1,
    )
    returned = lax.all_to_all(results, ("group", "local"), split_axis=0, concat_axis=0, tiled=True)
    spread = jnp.where(pick, weight_te.T[:, None, :], 0.0).reshape(experts * CAP, rows)
    high = spread.astype(jnp.bfloat16)
    low = (spread - high.astype(jnp.float32)).astype(jnp.bfloat16)
    both = jnp.concatenate([high, low], axis=1)
    out = []
    for q in range(4):
        back = returned[:, q * CAP:(q + 1) * CAP].reshape(experts * CAP, quarter)
        total = lax.dot_general(both, back, (((0,), (0,)), ((), ())), preferred_element_type=jnp.float32)
        out.append((total[:rows] + total[rows:]).astype(jnp.bfloat16))
    return jnp.concatenate(out, axis=1)


def solution(mesh):
    spec = P(("group", "local"), None)
    wide = P(("group", "local"), None, None)
    return jax.shard_map(
        body, mesh=mesh, in_specs=(spec, spec, spec, wide, wide, wide), out_specs=spec, check_vma=False
    )
```

profile of v0, /device:TPU:26, one launch (start us, length us, event | category | flops | bytes accessed | tf_op | source)
XLA Modules:
  0.0 408.4 jit_solution(3491581973890599466)
XLA Ops:
  6.4 4.3 %pad_maximum_fusion = bf16[128,40,896]{2,0,1:T(8,128)(2,1)} fusion(bf16[128,10,896]{2,0,1:T(8,128)(2,1)S(1)} %fusion.11, bf16[128,10,896]{2,0,1:T(8,128)(2,1)S(1)} %fusion.12, bf16[128,10,896]{2,0,1:T(8,128)(2,1)S(1)} %fusion.13, bf16[128,10,896]{2,0,1:T(8,128)(2,1)S(1)} %fusion.14), kind=kLoop, calls=%fused_computation | loop fusion | flops 13762560 | bytes 18350080 | tf_op jit(solution)/shard_map/concatenate | solution.py:27
  10.7 12.4 %copy.40 = bf16[128,40,896]{2,1,0:T(8,128)(2,1)} copy(bf16[128,40,896]{2,0,1:T(8,128)(2,1)} %pad_maximum_fusion) | data formatting | bytes 18350080 | tf_op jit(solution)/shard_map/concatenate | solution.py:27
  23.1 113.6 %all_to_all.10 = bf16[128,40,896]{2,1,0:T(8,128)(2,1)S(1)} all-to-all(bf16[128,40,896]{2,1,0:T(8,128)(2,1)} %copy.40), channel_id=1, replica_groups=mesh['group'=16,'local'=8] {'group','local'}, dimensions={0} | all-to-all | bytes 18350080 | tf_op jit(solution)/shard_map/all_to_all | solution.py:27
  136.8 7.3 %fusion.39 = (bf16[128,10,896]{2,1,0:T(8,128)(2,1)}, bf16[128,10,896]{2,1,0:T(8,128)(2,1)}, bf16[128,10,896]{2,1,0:T(8,128)(2,1)}, bf16[128,10,896]{2,1,0:T(8,128)(2,1)}) fusion(bf16[128,40,896]{2,1,0:T(8,128)(2,1)S(1)} %all_to_all.10), kind=kLoop, calls=%fused_computation.61 | loop fusion | bytes 18350080 | tf_op jit(solution)/shard_map/slice | solution.py:29
  144.1 3.9 reshape.78
  148.0 5.3 %reshape.77 = bf16[1280,896]{1,0:T(8,128)(2,1)} reshape(bf16[128,10,896]{2,1,0:T(8,128)(2,1)} %get-tuple-element.10) | data formatting | bytes 4587520 | tf_op jit(solution)/shard_map/reshape | solution.py:29
  153.3 5.3 %reshape.76 = bf16[1280,896]{1,0:T(8,128)(2,1)} reshape(bf16[128,10,896]{2,1,0:T(8,128)(2,1)} %get-tuple-element.11) | data formatting | bytes 4587520 | tf_op jit(solution)/shard_map/reshape | solution.py:29
  158.7 5.4 %reshape.75 = bf16[1280,896]{1,0:T(8,128)(2,1)} reshape(bf16[128,10,896]{2,1,0:T(8,128)(2,1)} %get-tuple-element.12) | data formatting | bytes 4587520 | tf_op jit(solution)/shard_map/reshape | solution.py:29
  169.6 11.3 %fusion = f32[1280,1024]{1,0:T(8,128)} fusion(bf16[1280,3584]{1,0:T(8,128)(2,1)S(1)} %constant_dynamic-update-slice_fusion, bf16[1,3584,1024]{2,1,0:T(8,128)(2,1)S(1)} %bitcast.36), kind=kOutput, calls=%fused_computation.2 | convolution fusion | flops 9395240960 | bytes 21757952 | tf_op jit(solution)/shard_map/dot_general | solution.py:32
  180.9 12.2 %multiply_convert_fusion = bf16[1280,1024]{1,0:T(8,128)(2,1)S(1)} fusion(f32[1280,1024]{1,0:T(8,128)} %fusion, bf16[1280,3584]{1,0:T(8,128)(2,1)S(1)} %constant_dynamic-update-slice_fusion, bf16[1,3584,1024]{2,1,0:T(8,128)(2,1)S(1)} %bitcast.38), kind=kOutput, calls=%fused_computation.6 | convolution fusion | flops 9403105280 | bytes 24379392 | tf_op jit(solution)/shard_map/dot_general | solution.py:31
  193.1 5.6 %convolution_convert_fusion = bf16[1280,896]{1,0:T(8,128)(2,1)} fusion(bf16[1280,1024]{1,0:T(8,128)(2,1)S(1)} %multiply_convert_fusion, bf16[1024,3584]{1,0:T(8,128)(2,1)} %bitcast.39), kind=kOutput, calls=%fused_computation.7 | convolution fusion | flops 2349957120 | bytes 6750208 | tf_op jit(solution)/shard_map/dot_general | solution.py:36
  198.7 5.6 %convolution_convert_fusion.1 = bf16[1280,896]{1,0:T(8,128)(2,1)} fusion(bf16[1280,1024]{1,0:T(8,128)(2,1)S(1)} %multiply_convert_fusion, bf16[1024,3584]{1,0:T(8,128)(2,1)} %bitcast.40), kind=kOutput, calls=%fused_computation.8 | convolution fusion | flops 2349957120 | bytes 6750208 | tf_op jit(solution)/shard_map/dot_general | solution.py:36
  204.3 4.6 %convolution_convert_fusion.2 = bf16[1280,896]{1,0:T(8,128)(2,1)S(1)} fusion(bf16[1280,1024]{1,0:T(8,128)(2,1)S(1)} %multiply_convert_fusion, bf16[1024,3584]{1,0:T(8,128)(2,1)} %bitcast.41), kind=kOutput, calls=%fused_computation.9 | convolution fusion | flops 2349957120 | bytes 6750208 | tf_op jit(solution)/shard_map/dot_general | solution.py:36
  208.8 5.7 %convolution_convert_fusion.3 = bf16[1280,896]{1,0:T(8,128)(2,1)} fusion(bf16[1280,1024]{1,0:T(8,128)(2,1)S(1)} %multiply_convert_fusion, bf16[1024,3584]{1,0:T(8,128)(2,1)} %bitcast.42), kind=kOutput, calls=%fused_computation.10 | convolution fusion | flops 2349957120 | bytes 6750208 | tf_op jit(solution)/shard_map/dot_general | solution.py:36
  214.5 5.2 %reshape.82 = bf16[128,10,896]{2,1,0:T(8,128)(2,1)} reshape(bf16[1280,896]{1,0:T(8,128)(2,1)} %convolution_convert_fusion) | data formatting | bytes 4587520 | tf_op jit(solution)/shard_map/reshape | solution.py:38
  219.6 5.2 %reshape.81 = bf16[128,10,896]{2,1,0:T(8,128)(2,1)} reshape(bf16[1280,896]{1,0:T(8,128)(2,1)} %convolution_convert_fusion.1) | data formatting | bytes 4587520 | tf_op jit(solution)/shard_map/reshape | solution.py:38
  224.8 5.2 %reshape.79 = bf16[128,10,896]{2,1,0:T(8,128)(2,1)} reshape(bf16[1280,896]{1,0:T(8,128)(2,1)} %convolution_convert_fusion.3) | data formatting | bytes 4587520 | tf_op jit(solution)/shard_map/reshape | solution.py:38
  232.7 12.8 %pad_maximum_fusion.1 = bf16[128,40,896]{2,1,0:T(8,128)(2,1)} fusion(bf16[128,10,896]{2,1,0:T(8,128)(2,1)} %reshape.82, bf16[128,10,896]{2,1,0:T(8,128)(2,1)} %reshape.81, bf16[128,10,896]{2,1,0:T(8,128)(2,1)} %reshape.80, bf16[128,10,896]{2,1,0:T(8,128)(2,1)} %reshape.79), kind=kLoop, calls=%fused_computation.1 | loop fusion | flops 36700160 | bytes 18350080 | tf_op jit(solution)/shard_map/concatenate | solution.py:34
  245.5 8.8 %all-to-all-start.1 = ((bf16[128,40,896]{2,1,0:T(8,128)(2,1)}), bf16[128,40,896]{2,1,0:T(8,128)(2,1)}, u32[]{:S(2)}, u32[]{:S(2)}) async-start(bf16[128,40,896]{2,1,0:T(8,128)(2,1)} %pad_maximum_fusion.1), calls=%async_computation.1 | async-start | bytes 18350080 | tf_op jit(solution)/shard_map/all_to_all | solution.py:43
  256.5 113.2 %all-to-all-done.1 = bf16[128,40,896]{2,1,0:T(8,128)(2,1)} async-done(((bf16[128,40,896]{2,1,0:T(8,128)(2,1)}), bf16[128,40,896]{2,1,0:T(8,128)(2,1)}, u32[]{:S(2)}, u32[]{:S(2)}) %all-to-all-start.1) | async-done | bytes 9175072 | tf_op jit(solution)/shard_map/all_to_all | solution.py:43
  369.7 11.9 %fusion.38 = (bf16[128,10,896]{2,1,0:T(8,128)(2,1)}, bf16[128,10,896]{2,1,0:T(8,128)(2,1)}, bf16[128,10,896]{2,1,0:T(8,128)(2,1)}, bf16[128,10,896]{2,1,0:T(8,128)(2,1)}) fusion(bf16[128,40,896]{2,1,0:T(8,128)(2,1)} %all-to-all-done.1), kind=kLoop, calls=%fused_computation.60 | loop fusion | bytes 18350080 | tf_op jit(solution)/shard_map/slice | solution.py:50
  381.6 3.9 reshape.83
  385.5 5.3 %reshape.86 = bf16[1280,896]{1,0:T(8,128)(2,1)} reshape(bf16[128,10,896]{2,1,0:T(8,128)(2,1)} %get-tuple-element.6) | data formatting | bytes 4587520 | tf_op jit(solution)/shard_map/reshape | solution.py:50
  394.6 3.9 reshape.85
  (58 shorter events, 30.3 us)
Async XLA Ops:
  0.0 4.8 %copy-start.3 = (bf16[128,3584]{1,0:T(8,128)(2,1)S(1)}, bf16[128,3584]{1,0:T(8,128)(2,1)}, u32[]{:S(2)}) copy-start(bf16[128,3584]{1,0:T(8,128)(2,1)} %param.6) | copy-start | bytes 2752516
  164.1 2.3 copy-start.1
  164.1 3.0 copy-start
  166.4 2.4 slice-start
  167.1 2.5 slice-start.1
  167.4 13.5 %slice-start.2 = ((s8[7340032]{0:T(1024)(128)(4,1)}), s8[4194304]{0:T(1024)(128)(4,1)S(1)}, s32[]{:S(2)}) async-start(s8[7340032]{0:T(1024)(128)(4,1)} %bitcast.37), calls=%async_computation.4 | async-start | bytes 8388608
  169.6 11.3 %slice-start.3 = ((s8[7340032]{0:T(1024)(128)(4,1)}), s8[3145728]{0:T(1024)(128)(4,1)S(1)}, s32[]{:S(2)}) async-start(s8[7340032]{0:T(1024)(128)(4,1)} %bitcast.37), calls=%async_computation.5 | async-start | bytes 6291456
  245.5 8.9 %copy-start.7 = (f32[128,8]{0,1:T(8,128)S(1)}, f32[128,8]{0,1:T(8,128)}, u32[]{:S(2)}) copy-start(f32[128,8]{0,1:T(8,128)} %param.8) | copy-start | bytes 12292
  245.5 124.3 %all-to-all-start.1 = ((bf16[128,40,896]{2,1,0:T(8,128)(2,1)}), bf16[128,40,896]{2,1,0:T(8,128)(2,1)}, u32[]{:S(2)}, u32[]{:S(2)}) async-start(bf16[128,40,896]{2,1,0:T(8,128)(2,1)} %pad_maximum_fusion.1), calls=%async_computation.1 | async-start | bytes 18350080 | tf_op jit(solution)/shard_map/all_to_all | solution.py:43
  390.8 2.0 copy-start.2
  390.8 2.0 copy-start.6
  405.2 2.0 copy-start.4
  405.2 2.0 copy-start.5
where the time goes:
time: 410 us; the launch traced here: 408 us
  blocking collectives  114 us (28%)
  waiting for transfers between devices  113 us (28%)
  local copies, waits for them, and re-layouts  93.9 us (23%)
  matrix products  58.4 us (14%)
  other arithmetic  20.1 us (5%)
  starting transfers between devices  8.84 us (2%)
    all_to_all x1, blocking collectives, body(): lax.all_to_all(jnp.concatenate(parts, axis=1), ('group', 'local'), split_...  114 us
    all_to_all x1, waiting for transfers between devices, body(): lax.all_to_all(results, ('group', 'local'), split_axis=0, concat_axis=0,...  113 us
    dot_general x4, matrix products, body(): jnp.dot(hidden, w_down[0][:, q * quarter:(q + 1) * quarter], preferred_el...  21.4 us
    reshape x4, local copies, waits for them, and re-layouts, body(): arrived[:, q * CAP:(q + 1) * CAP].reshape(experts * CAP, quarter)  19.9 us
    reshape x4, local copies, waits for them, and re-layouts, body(): results = jnp.concatenate([jnp.dot(hidden, w_down[0][:, q * quarter:(q +...  18.2 us
    reshape x4, local copies, waits for them, and re-layouts, body(): back = returned[:, q * CAP:(q + 1) * CAP].reshape(experts * CAP, quarter)  17.1 us
    concatenate x1, other arithmetic, body(): jnp.concatenate([jnp.dot(hidden, w_down[0][:, q * quarter:(q + 1) * quart...  12.8 us
    concatenate x1, local copies, waits for them, and re-layouts, body(): jnp.concatenate(parts, axis=1)  12.4 us
  transfers between devices with their start and end apart: 1, of which 1 were waited for; matrix products, arithmetic and copies ran while one was open for 1% of the time, Pallas kernels for 0%

commit v1 on v0

v1 whole, which is shorter than its diff:
```python
import functools

import jax
import jax.numpy as jnp
from jax import lax
from jax.experimental import pallas as pl
from jax.experimental.pallas import tpu as pltpu
from jax.sharding import PartitionSpec as P

CAP = 10
SIDE = 4
CORES = 2
BLOCK = SIDE * CAP
SLOTS = SIDE * CORES * BLOCK
LANES = 384
ORDERS = ((0, 1, 2), (1, 2, 0), (2, 0, 1))
WIDTHS = (1152, 1280, 1152)
STARTS = (0, 1152, 2432)
TILES = (384, 256, 384)
RING = (1, 3, 2)
BF16 = jnp.bfloat16
F32 = jnp.float32


def whereabouts():
    group, local = lax.axis_index("group"), lax.axis_index("local")
    return (group // SIDE, group % SIDE, local // CORES), local % CORES


def device_at(pos, core):
    return (pos[0] * SIDE + pos[1], pos[2] * CORES + core)


def along(pos, axis, value):
    return tuple(value if a == axis else pos[a] for a in range(3))


def greet(pos, core):
    barrier = pltpu.get_barrier_semaphore()
    peers = [device_at(pos, 1 - core)]
    for axis in range(3):
        for step in RING:
            for other in range(CORES):
                there = along(pos, axis, (pos[axis] + step) % SIDE)
                peers.append(device_at(there, (core + other) % CORES))
    for peer in peers:
        pl.semaphore_signal(barrier, inc=1, device_id=peer, device_id_type=pl.DeviceIdType.MESH)
    pl.semaphore_wait(barrier, len(peers))


def send(src, dst, send_sem, recv_sem, device):
    return pltpu.make_async_remote_copy(
        src_ref=src, dst_ref=dst, send_sem=send_sem, recv_sem=recv_sem,
        device_id=device, device_id_type=pl.DeviceIdType.MESH,
    )


LAST = tuple((step, other) for step in RING for other in range(CORES)) + ((0, 1),)


def dispatch_kernel(tok, meta, xa, xb, xc, mixed, ga, gb, gc, sa, sb, sc, ra, rb, rc, notes, picks,
                    s1, r1, sm, rm, s2, r2, s3, r3, keep):
    pos, core = whereabouts()
    outs, gathered, cut, relay = (xa, xb, xc), (ga, gb, gc), (sa, sb, sc), (ra, rb, rc)
    greet(pos, core)
    first = []
    for step in RING:
        for p, (a1, _, _) in enumerate(ORDERS):
            there = (pos[a1] + step) % SIDE
            peer = device_at(along(pos, a1, there), core)
            first.append(send(meta.at[p, there], notes.at[p, pos[a1]], sm.at[p, step], rm.at[p, pos[a1]], peer))
            first[-1].start()
            columns = pl.ds(STARTS[p], WIDTHS[p])
            first.append(send(tok.at[:, columns], gathered[p].at[pos[a1]], s1.at[p, step], r1.at[p, pos[a1]], peer))
            first[-1].start()
    for p, (a1, _, _) in enumerate(ORDERS):
        gathered[p][pos[a1]] = tok[:, STARTS[p]:STARTS[p] + WIDTHS[p]]
        notes[p, pos[a1]] = meta[p, pos[a1]]

    second, third, local = [], [], []

    def forward(p, step):
        a1, a2, a3 = ORDERS[p]
        origin = (pos[a2] + step) % SIDE
        source = cut[p] if step == 0 else relay[p]
        mine = pos[a3] * CORES + core
        for j, (way, other) in enumerate(LAST):
            there = (pos[a3] + way) % SIDE
            side = (core + other) % CORES
            third.append(send(
                source.at[origin, there * CORES + side], outs[p].at[mine, origin],
                s3.at[p, step, j], r3.at[p, origin, mine], device_at(along(pos, a3, there), side),
            ))
            third[-1].start()
        local.append(pltpu.make_async_copy(source.at[origin, mine], outs[p].at[mine, origin], keep.at[p, step]))
        local[-1].start()

    for p, (a1, a2, a3) in enumerate(ORDERS):
        for step in RING:
            there = (pos[a1] + step) % SIDE
            peer = device_at(along(pos, a1, there), core)
            send(meta.at[p, there], notes.at[p, there], sm.at[p, step], rm.at[p, there], peer).wait_recv()
            columns = pl.ds(STARTS[p], WIDTHS[p])
            send(tok.at[:, columns], gathered[p].at[there], s1.at[p, step], r1.at[p, there], peer).wait_recv()
        largest = jnp.maximum(jnp.maximum(notes[p, 0], notes[p, 1]), jnp.maximum(notes[p, 2], notes[p, 3]))
        total = notes[p, 0] + notes[p, 1] + notes[p, 2] + notes[p, 3]
        row = lax.broadcasted_iota(jnp.int32, (8, LANES), 0)
        table = jnp.where(row < SIDE, largest, total)
        mixed[p] = table
        turned = table.T
        place = lax.broadcasted_iota(jnp.int32, (SLOTS, SIDE * 128), 1).astype(F32)
        for there in range(SIDE):
            picks[there] = (turned[:SLOTS, there:there + 1] == place).astype(BF16)
        for step in RING + (0,):
            there = (pos[a2] + step) % SIDE

            @pl.loop(0, WIDTHS[p] // TILES[p])
            def _(n):
                columns = pl.ds(pl.multiple_of(n * TILES[p], 128), TILES[p])
                rows = gathered[p][:, :, columns].reshape(SIDE * 128, TILES[p])
                found = jnp.dot(picks[there], rows, preferred_element_type=F32)
                for d in range(SIDE * CORES):
                    cut[p][there, d, :, columns] = found[d * BLOCK:(d + 1) * BLOCK].astype(BF16)

            if step:
                second.append(send(
                    cut[p].at[there], relay[p].at[pos[a2]], s2.at[p, step], r2.at[p, pos[a2]],
                    device_at(along(pos, a2, there), core),
                ))
                second[-1].start()
            else:
                forward(p, 0)
    for step in (3, 1, 2):
        for p, (a1, a2, a3) in enumerate(ORDERS):
            there = (pos[a2] + step) % SIDE
            send(
                cut[p].at[there], relay[p].at[there], s2.at[p, step], r2.at[p, there],
                device_at(along(pos, a2, there), core),
            ).wait_recv()
            forward(p, step)
    for p, (a1, a2, a3) in enumerate(ORDERS):
        for step in range(SIDE):
            origin = (pos[a2] + step) % SIDE
            for j, (way, other) in enumerate(LAST):
                there = (pos[a3] + way) % SIDE
                side = (core + other) % CORES
                from_d = there * CORES + side
                send(
                    cut[p].at[origin, from_d], outs[p].at[from_d, origin],
                    s3.at[p, step, j], r3.at[p, origin, from_d], device_at(along(pos, a3, there), side),
                ).wait_recv()
    for copy in first + second + third:
        copy.wait_send()
    for copy in local:
        copy.wait()


def return_kernel(ya, yb, yc, mixed, out, la, lb, lc, ha, hb, hc, pa, pb, pc, qa, qb, qc, spread,
                  s3, r3, s2, r2, s1, r1, keep):
    pos, core = whereabouts()
    results, landed, home, parts, others = (ya, yb, yc), (la, lb, lc), (ha, hb, hc), (pa, pb, pc), (qa, qb, qc)
    greet(pos, core)
    sent, local = [], []
    for step in RING + (0,):
        for p, (a1, a2, a3) in enumerate(ORDERS):
            owner = (pos[a2] + step) % SIDE
            mine = pos[a3] * CORES + core
            for j, (way, other) in enumerate(LAST):
                there = (pos[a3] + way) % SIDE
                side = (core + other) % CORES
                sent.append(send(
                    results[p].at[there * CORES + side, owner], landed[p].at[owner, mine],
                    s3.at[p, step, j], r3.at[p, owner, mine], device_at(along(pos, a3, there), side),
                ))
                sent[-1].start()
            local.append(pltpu.make_async_copy(
                results[p].at[mine, owner], landed[p].at[owner, mine], keep.at[p, step]
            ))
            local[-1].start()
    local_at = 0
    for step in RING + (0,):
        for p, (a1, a2, a3) in enumerate(ORDERS):
            owner = (pos[a2] + step) % SIDE
            for j, (way, other) in enumerate(LAST):
                there = (pos[a3] + way) % SIDE
                side = (core + other) % CORES
                from_d = there * CORES + side
                send(
                    results[p].at[from_d, owner], landed[p].at[owner, from_d],
                    s3.at[p, step, j], r3.at[p, owner, from_d], device_at(along(pos, a3, there), side),
                ).wait_recv()
            local[local_at].wait()
            local_at += 1
            if step:
                sent.append(send(
                    landed[p].at[owner], home[p].at[pos[a2]], s2.at[p, step], r2.at[p, pos[a2]],
                    device_at(along(pos, a2, owner), core),
                ))
                sent[-1].start()
    for p, (a1, a2, a3) in enumerate(ORDERS):
        token = lax.broadcasted_iota(jnp.int32, (SIDE * 128, SLOTS), 0).astype(F32)
        for there in range(SIDE):
            index = mixed[p, there:there + 1, :SLOTS]
            weight = mixed[p, SIDE + there:SIDE + there + 1, :SLOTS]
            spread[there] = jnp.where(token == index, weight, 0.0).astype(BF16)
        for step in RING:
            there = (pos[a2] + step) % SIDE
            send(
                landed[p].at[there], home[p].at[there], s2.at[p, step], r2.at[p, there],
                device_at(along(pos, a2, there), core),
            ).wait_recv()

        @pl.loop(0, WIDTHS[p] // TILES[p])
        def _(n):
            columns = pl.ds(pl.multiple_of(n * TILES[p], 128), TILES[p])
            total = jnp.zeros((SIDE * 128, TILES[p]), F32)
            for step in range(SIDE):
                there = (pos[a2] + step) % SIDE
                source = home[p] if step else landed[p]
                rows = source[there, :, :, columns].astype(F32).reshape(SLOTS, TILES[p]).astype(BF16)
                total = total + jnp.dot(spread[there], rows, preferred_element_type=F32)
            for k in range(SIDE):
                parts[p][k, :, columns] = total[k * 128:(k + 1) * 128].astype(BF16)

        for step in RING:
            there = (pos[a1] + step) % SIDE
            sent.append(send(
                parts[p].at[there], others[p].at[pos[a1]], s1.at[p, step], r1.at[p, pos[a1]],
                device_at(along(pos, a1, there), core),
            ))
            sent[-1].start()
    for p, (a1, a2, a3) in enumerate(ORDERS):
        total = parts[p][pos[a1]].astype(F32)
        for step in RING:
            there = (pos[a1] + step) % SIDE
            send(
                parts[p].at[there], others[p].at[there], s1.at[p, step], r1.at[p, there],
                device_at(along(pos, a1, there), core),
            ).wait_recv()
            total = total + others[p][there].astype(F32)
        out[:, STARTS[p]:STARTS[p] + WIDTHS[p]] = total.astype(BF16)
    for copy in sent:
        copy.wait_send()


def expert_kernel(xa, xb, xc, wg, wu, wd, turn, ya, yb, yc, va, vb, vc, gate_w, up_w, down_w, turns, full, hid, hid_a, hid_c,
                  xsem, wsem, ysem):
    arrived, held, results = (xa, xb, xc), (va, vb, vc), (ya, yb, yc)
    loads = [pltpu.make_async_copy(turn, turns, wsem.at[3])]
    loads += [pltpu.make_async_copy(arrived[p], held[p], xsem.at[p]) for p in range(3)]
    weights = [pltpu.make_async_copy(a, b, wsem.at[i]) for i, (a, b) in enumerate(((wg, gate_w), (wu, up_w), (wd, down_w)))]
    for copy in loads + weights:
        copy.start()
    for copy in loads:
        copy.wait()
    stores = []
    for side in range(CORES):
        for p in range(3):
            @pl.loop(0, WIDTHS[p] // TILES[p])
            def _(n):
                columns = pl.ds(pl.multiple_of(n * TILES[p], 128), TILES[p])
                rows = held[p][:, side, :, columns].reshape(SIDE * SIDE * BLOCK, TILES[p])
                if p != 1:
                    rows = jnp.dot(turns[p // 2], rows, preferred_element_type=F32).astype(BF16)
                full[:, pl.ds(pl.multiple_of(STARTS[p] + n * TILES[p], 128), TILES[p])] = rows
        if side == 0:
            weights[0].wait()
            weights[1].wait()

        @pl.loop(0, 4)
        def _(n):
            columns = pl.ds(pl.multiple_of(n * 256, 128), 256)
            gate = jnp.dot(full[...], gate_w[:, columns], preferred_element_type=F32)
            lin = jnp.dot(full[...], up_w[:, columns], preferred_element_type=F32)
            hid[:, columns] = (gate * (1.0 / (1.0 + jnp.exp(-gate))) * lin).astype(BF16)

        @pl.loop(0, 4)
        def _(n):
            columns = pl.ds(pl.multiple_of(n * 256, 128), 256)
            hid_a[:, columns] = jnp.dot(turns[1], hid[:, columns], preferred_element_type=F32).astype(BF16)
            hid_c[:, columns] = jnp.dot(turns[0], hid[:, columns], preferred_element_type=F32).astype(BF16)

        if side == 0:
            weights[2].wait()
        for p, rows in enumerate((hid_a, hid, hid_c)):
            @pl.loop(0, WIDTHS[p] // TILES[p])
            def _(n):
                columns = pl.ds(pl.multiple_of(n * TILES[p], 128), TILES[p])
                of_w = pl.ds(pl.multiple_of(STARTS[p] + n * TILES[p], 128), TILES[p])
                result = jnp.dot(rows[...], down_w[:, of_w], preferred_element_type=F32).astype(BF16)
                held[p][:, side, :, columns] = result.reshape(SIDE, SIDE * BLOCK, TILES[p])

            stores.append(pltpu.make_async_copy(held[p].at[:, side], results[p].at[:, side], ysem.at[p, side]))
            stores[-1].start()
    for copy in stores:
        copy.wait()


ANY = pl.BlockSpec(memory_space=pl.ANY)
VMEM = pl.BlockSpec(memory_space=pltpu.VMEM)
DMA = pltpu.SemaphoreType.DMA


def blocks(leading):
    return [jax.ShapeDtypeStruct(leading + (w,), BF16) for w in WIDTHS]


def scratch(leading):
    return [pltpu.VMEM(leading + (w,), BF16) for w in WIDTHS]


def turn_matrices():
    row = jnp.arange(SIDE * SIDE * BLOCK, dtype=jnp.int32)
    k, i, j, s = row // 160, row // 40 % 4, row // 10 % 4, row % 10
    there = (i * 160 + j * 40 + k * 10 + s)[:, None] == row[None, :]
    return jnp.stack([there, there.T]).astype(BF16)


def tables(expert_ids, gate_weights):
    rows = expert_ids.shape[0]
    experts = SIDE ** 3 * CORES
    hit = expert_ids[:, :, None] == jnp.arange(experts, dtype=jnp.int32)[None, None, :]
    named = jnp.any(hit, axis=1)
    weight = jnp.sum(jnp.where(hit, gate_weights[:, :, None], 0.0), axis=1)
    below = (jnp.arange(rows)[:, None] > jnp.arange(rows)[None, :]).astype(BF16)
    place = jnp.dot(below, named.astype(BF16), preferred_element_type=F32).astype(jnp.int32)
    place = jnp.where(named, place, -1)
    pick = place.T[:, None, :] == jnp.arange(CAP, dtype=jnp.int32)[None, :, None]
    token = jnp.max(jnp.where(pick, jnp.arange(rows, dtype=jnp.int32).astype(F32)[None, None, :], -1.0), axis=2)
    amount = jnp.sum(jnp.where(pick, weight.T[:, None, :], 0.0), axis=2)
    shape = (SIDE, SIDE, SIDE, CORES, CAP)
    token, amount = token.reshape(shape), amount.reshape(shape)
    pos, _ = whereabouts()
    made = []
    for a1, a2, a3 in ORDERS:
        mine = (jnp.arange(SIDE) == pos[a1])[None, None, None, None, :, None]
        order = (a1, a2, a3, 3, 4)
        index = token.transpose(order)[:, :, :, :, None, :]
        index = jnp.where(mine & (index >= 0), index + (128 * pos[a1]).astype(F32), -1.0)
        value = jnp.where(mine, amount.transpose(order)[:, :, :, :, None, :], 0.0)
        index = jnp.pad(index.reshape(SIDE, SIDE, SLOTS), ((0, 0), (0, 0), (0, LANES - SLOTS)), constant_values=-1.0)
        value = jnp.pad(value.reshape(SIDE, SIDE, SLOTS), ((0, 0), (0, 0), (0, LANES - SLOTS)))
        made.append(jnp.concatenate([index, value], axis=1))
    return jnp.stack(made)


def body(tokens, expert_ids, gate_weights, w_gate, w_up, w_down):
    meta = tables(expert_ids, gate_weights)
    params = functools.partial(pltpu.CompilerParams, vmem_limit_bytes=60 * 2 ** 20)
    D8 = SIDE * CORES
    *arrived, mixed = pl.pallas_call(
        dispatch_kernel,
        out_shape=blocks((D8, SIDE, BLOCK)) + [jax.ShapeDtypeStruct((3, 8, LANES), F32)],
        in_specs=[VMEM, VMEM],
        out_specs=[ANY, ANY, ANY, VMEM],
        scratch_shapes=scratch((SIDE, 128)) + scratch((SIDE, D8, BLOCK)) + scratch((SIDE, D8, BLOCK)) + [
            pltpu.VMEM((3, SIDE, 8, LANES), F32),
            pltpu.VMEM((SIDE, SLOTS, SIDE * 128), BF16),
        ] + [DMA((3, SIDE))] * 6 + [DMA((3, SIDE, 7)), DMA((3, SIDE, D8)), DMA((3, SIDE))],
        compiler_params=params(collective_id=0, has_side_effects=True),
        name="dispatch",
    )(tokens, meta)
    arrived = [a.reshape(SIDE, CORES, SIDE * BLOCK, a.shape[-1]) for a in arrived]
    half = SIDE * SIDE * BLOCK
    results = pl.pallas_call(
        expert_kernel,
        out_shape=blocks((SIDE, CORES, SIDE * BLOCK)),
        in_specs=[ANY] * 7,
        out_specs=[ANY] * 3,
        scratch_shapes=scratch((SIDE, CORES, SIDE * BLOCK)) + [
            pltpu.VMEM(w_gate.shape[1:], BF16), pltpu.VMEM(w_up.shape[1:], BF16), pltpu.VMEM(w_down.shape[1:], BF16),
            pltpu.VMEM((2, half, half), BF16),
            pltpu.VMEM((half, tokens.shape[1]), BF16),
        ] + [pltpu.VMEM((half, w_gate.shape[2]), BF16)] * 3 + [DMA((3,)), DMA((4,)), DMA((3, CORES))],
        compiler_params=params(),
        name="expert",
    )(*arrived, w_gate[0], w_up[0], w_down[0], turn_matrices())
    results = [r.reshape(D8, SIDE, BLOCK, r.shape[-1]) for r in results]
    return pl.pallas_call(
        return_kernel,
        out_shape=jax.ShapeDtypeStruct(tokens.shape, BF16),
        in_specs=[ANY] * 3 + [VMEM],
        out_specs=VMEM,
        scratch_shapes=scratch((SIDE, D8, BLOCK)) + scratch((SIDE, D8, BLOCK)) + scratch((SIDE, 128)) + scratch((SIDE, 128)) + [
            pltpu.VMEM((SIDE, SIDE * 128, SLOTS), BF16),
        ] + [DMA((3, SIDE, 7)), DMA((3, SIDE, D8))] + [DMA((3, SIDE))] * 5,
        compiler_params=params(collective_id=1, has_side_effects=True),
        name="give_back",
    )(*results, mixed)


def solution(mesh):
    spec = P(("group", "local"), None)
    wide = P(("group", "local"), None, None)
    return jax.shard_map(
        body, mesh=mesh, in_specs=(spec, spec, spec, wide, wide, wide), out_specs=spec, check_vma=False
    )
```

time: 410 us -> 275 us (0.67)
  Pallas kernels: 0 us -> 260 us
  blocking collectives: 114 us -> 0 us
  waiting for transfers between devices: 113 us -> 0 us
  local copies, waits for them, and re-layouts: 93.9 us -> 8.04 us
  matrix products: 58.4 us -> 0.19 us
  other arithmetic: 20.1 us -> 3.93 us
  starting transfers between devices: 8.84 us -> 0 us
    pallas_call x0 -> x3, Pallas kernels: none -> 260 us  [the longest x1 103 us: body(): pl.pallas_call(dispatch_kernel, out_shape=blocks((D8, SIDE, BLOCK)) + [ja...]
    all_to_all x1 -> x0, blocking collectives: 114 us -> none  [body(): lax.all_to_all(jnp.concatenate(parts, axis=1), ('group', 'local'), split_...]
    all_to_all x1 -> x0, waiting for transfers between devices: 113 us -> none  [body(): lax.all_to_all(results, ('group', 'local'), split_axis=0, concat_axis=0,...]
    dot_general x15 -> x1, matrix products: 58.4 us -> 0.19 us  [tables(): jnp.dot(below, named.astype(BF16), preferred_element_type=F32)]
    reshape x12 -> x0, local copies, waits for them, and re-layouts: 55.2 us -> none  [the longest x4 19.9 us: body(): arrived[:, q * CAP:(q + 1) * CAP].reshape(experts * CAP, quarter)]
    slice x2 -> x0, local copies, waits for them, and re-layouts: 19.2 us -> none  [the longest x1 11.9 us: body(): back = returned[:, q * CAP:(q + 1) * CAP].reshape(experts * CAP, quarter)]
    concatenate x3 -> x0, other arithmetic: 18.1 us -> none  [the longest x1 12.8 us: body(): jnp.concatenate([jnp.dot(hidden, w_down[0][:, q * quarter:(q + 1) * quart...]
    concatenate x2 -> x0, local copies, waits for them, and re-layouts: 12.8 us -> none  [the longest x1 12.4 us: body(): jnp.concatenate(parts, axis=1)]
  transfers between devices with their start and end apart: 1 -> 0, of which waited for: 1 -> 0; matrix products, arithmetic and copies ran while one was open for 1% -> 0% of each run, Pallas kernels for 0% -> 0%
where the time goes in v1:
time: 275 us; the launch traced here: 273 us
  Pallas kernels  260 us (95%)
  local copies, waits for them, and re-layouts  8.04 us (3%)
  other arithmetic  3.93 us (1%)
    pallas_call x1, Pallas kernels, body(): pl.pallas_call(dispatch_kernel, out_shape=blocks((D8, SIDE, BLOCK)) + [ja...  103 us
    pallas_call x1, Pallas kernels, body(): pl.pallas_call(return_kernel, out_shape=jax.ShapeDtypeStruct(tokens.shape...  98.5 us
    pallas_call x1, Pallas kernels, body(): pl.pallas_call(expert_kernel, out_shape=blocks((SIDE, CORES, SIDE * BLOCK...  59 us

profile of v1, /device:TPU:26, one launch (start us, length us, event | category | flops | bytes accessed | tf_op | source)
XLA Modules:
  0.0 272.6 jit_solution(13336888429922914189)
XLA Ops:
  0.3 0.1 and.149
  0.6 0.8 copy.36
  1.4 0.3 fusion.1
  1.8 0.2 fusion
  2.0 0.8 copy.40
  2.8 0.3 select_reduce_fusion.2
  3.2 0.4 select_reduce_fusion.1
  3.7 0.1 copy.38
  4.0 0.2 and.152
  4.3 0.2 and.159
  4.9 0.2 and.145
  5.4 0.3 broadcast_in_dim.147
  5.7 0.3 broadcast_in_dim.151
  6.1 0.3 broadcast_in_dim.153
  6.4 0.3 broadcast_in_dim.149
  6.8 0.3 broadcast_in_dim.136
  7.2 0.3 broadcast_in_dim.144
  7.5 0.7 pad_maximum_fusion.meta
  8.2 0.6 iota_compare_fusion.1
  8.7 1.5 add_convert_fusion.turn
  10.2 102.7 %dispatch.1 = (bf16[8,4,40,1152]{3,2,1,0:T(8,128)(2,1)}, bf16[8,4,40,1280]{3,2,1,0:T(8,128)(2,1)}, bf16[8,4,40,1152]{3,2,1,0:T(8,128)(2,1)}, f32[3,8,384]{2,1,0:T(8,128)}) custom-call(bf16[128,3584]{1,0:T(8,128)(2,1)} %tok.1, f32[3,4,8,384]{3,2,1,0:T(8,128)} %pad_maximum_fusion.meta), custom_call_target="tpu_custom_call" | custom-call | tf_op jit(solution)/shard_map/dispatch/pallas_call | solution.py:351
  113.0 59.0 %expert.1 = (bf16[4,2,160,1152]{3,2,1,0:T(8,128)(2,1)}, bf16[4,2,160,1280]{3,2,1,0:T(8,128)(2,1)}, bf16[4,2,160,1152]{3,2,1,0:T(8,128)(2,1)}) custom-call(bf16[4,2,160,1152]{3,2,1,0:T(8,128)(2,1)} %bitcast.39, bf16[4,2,160,1280]{3,2,1,0:T(8,128)(2,1)} %bitcast.36, bf16[4,2,160,1152]{3,2,1,0:T(8,128)(2,1)} %bitcast.40, bf16[3584,1024]{1,0:T(8,128)(2,1)} %bitcast.32, ...), custom_call_target="tpu_custom_call" | custom-call | tf_op jit(solution)/shard_map/expert/pallas_call | solution.py:365
  171.9 98.5 %give_back.1 = bf16[128,3584]{1,0:T(8,128)(2,1)} custom-call(bf16[8,4,40,1152]{3,2,1,0:T(8,128)(2,1)} %bitcast.37, bf16[8,4,40,1280]{3,2,1,0:T(8,128)(2,1)} %bitcast.35, bf16[8,4,40,1152]{3,2,1,0:T(8,128)(2,1)} %bitcast.38, f32[3,8,384]{2,1,0:T(8,128)} %get-tuple-element.18.mixed), custom_call_target="tpu_custom_call" | custom-call | tf_op jit(solution)/shard_map/give_back/pallas_call | solution.py:379
  270.5 2.2 copy.53
  (39 shorter events, 2.0 us)

commit v2 on v0

v2 whole, which is shorter than its diff:
```python
import jax
import jax.numpy as jnp
from jax import lax
from jax.experimental import pallas as pl
from jax.experimental.pallas import tpu as pltpu
from jax.sharding import PartitionSpec as P

CAP = 10
SIDE = 4
CORES = 2
BLOCK = SIDE * CAP
SLOTS = SIDE * CORES * BLOCK
HALF = SIDE * SIDE * BLOCK
LANES = 384
ORDERS = ((0, 1, 2), (1, 2, 0), (2, 0, 1))
WIDTHS = (1152, 1280, 1152)
STARTS = (0, 1152, 2432)
TILES = (384, 256, 384)
RING = (1, 3, 2)
BF16 = jnp.bfloat16
F32 = jnp.float32


def whereabouts():
    group, local = lax.axis_index("group"), lax.axis_index("local")
    return (group // SIDE, group % SIDE, local // CORES), local % CORES


def device_at(pos, core):
    return (pos[0] * SIDE + pos[1], pos[2] * CORES + core)


def along(pos, axis, value):
    return tuple(value if a == axis else pos[a] for a in range(3))


def greet(pos, core):
    barrier = pltpu.get_barrier_semaphore()
    peers = [device_at(pos, 1 - core)]
    for axis in range(3):
        for step in RING:
            for other in range(CORES):
                there = along(pos, axis, (pos[axis] + step) % SIDE)
                peers.append(device_at(there, (core + other) % CORES))
    for peer in peers:
        pl.semaphore_signal(barrier, inc=1, device_id=peer, device_id_type=pl.DeviceIdType.MESH)
    pl.semaphore_wait(barrier, len(peers))


def send(src, dst, send_sem, recv_sem, device):
    return pltpu.make_async_remote_copy(
        src_ref=src, dst_ref=dst, send_sem=send_sem, recv_sem=recv_sem,
        device_id=device, device_id_type=pl.DeviceIdType.MESH,
    )


def layer_kernel(tok, meta, wg, wu, wd, turn, out, ra, rb, rc, la, lb, lc, ha, hb, hc,
                 ga, gb, gc, sa, sb, sc, xa, xb, xc, qa, qb, qc, gate_w, up_w, down_w, turns, full, hid, hid_t, notes, mixed,
                 wsem, s1, r1, sm, rm, s2, r2, s3, r3, keep, t3, u3, keep_t, t2, u2, fetch, t1, u1):
    pos, core = whereabouts()
    gathered, cut, relay, held = (ga, gb, gc), (sa, sb, sc), (ra, rb, rc), (xa, xb, xc)
    landed, home, others = (la, lb, lc), (ha, hb, hc), (qa, qb, qc)
    loads = [
        pltpu.make_async_copy(a, b, wsem.at[i])
        for i, (a, b) in enumerate(((turn, turns), (wg, gate_w), (wu, up_w), (wd, down_w)))
    ]
    for copy in loads:
        copy.start()
    greet(pos, core)

    def spot(p, stage, step):
        return (pos[ORDERS[p][stage]] + step) % SIDE

    def mine(p, stage):
        return pos[ORDERS[p][stage]]

    def peer(p, stage, step, other=0):
        return device_at(along(pos, ORDERS[p][stage], spot(p, stage, step)), (core + other) % CORES)

    def columns_of(p):
        return pl.ds(STARTS[p], WIDTHS[p])

    def tile(p, n, start=0):
        return pl.ds(pl.multiple_of(start + n * TILES[p], 128), TILES[p])

    def tables_out(p, step, slot):
        return send(meta.at[p, spot(p, 0, step)], notes.at[p, slot], sm.at[p, step], rm.at[p, slot], peer(p, 0, step))

    def tokens_out(p, step, slot):
        return send(
            tok.at[:, columns_of(p)], gathered[p].at[slot], s1.at[p, step], r1.at[p, slot], peer(p, 0, step)
        )

    def picked_out(p, step, h, slot):
        return send(
            cut[p].at[spot(p, 1, step), h], relay[p].at[slot, h], s2.at[p, step, h], r2.at[p, slot, h], peer(p, 1, step)
        )

    def block_source(p, step):
        return cut[p] if step == 0 else relay[p]

    def block_out(p, step, h, way, slot):
        origin = spot(p, 1, step)
        return send(
            block_source(p, step).at[origin, h, spot(p, 2, way)], held[p].at[h, slot, origin],
            s3.at[p, step, h, way], r3.at[p, origin, h, slot], peer(p, 2, way, h),
        )

    def block_kept(p, step):
        origin = spot(p, 1, step)
        return pltpu.make_async_copy(
            block_source(p, step).at[origin, 0, mine(p, 2)], held[p].at[0, mine(p, 2), origin], keep.at[p, step]
        )

    def result_out(p, step, h, way, slot):
        owner = spot(p, 1, step)
        return send(
            held[p].at[h, spot(p, 2, way), owner], landed[p].at[owner, h, slot],
            t3.at[p, step, h, way], u3.at[p, owner, h, slot], peer(p, 2, way, h),
        )

    def result_kept(p, step):
        owner = spot(p, 1, step)
        return pltpu.make_async_copy(
            held[p].at[0, mine(p, 2), owner], landed[p].at[owner, 0, mine(p, 2)], keep_t.at[p, step]
        )

    def result_on(p, step, h, slot):
        return send(
            landed[p].at[spot(p, 1, step), h], home[p].at[slot, h], t2.at[p, step, h], u2.at[p, slot, h], peer(p, 1, step)
        )

    def fetched(p, step, h):
        origin = spot(p, 1, step)
        source = home[p] if step else landed[p]
        return pltpu.make_async_copy(source.at[origin, h], cut[p].at[origin, h], fetch.at[p, step, h])

    def sum_out(p, step, slot):
        return send(
            gathered[p].at[spot(p, 0, step)], others[p].at[slot], t1.at[p, step], u1.at[p, slot], peer(p, 0, step)
        )

    def ways(h):
        return RING + (0,) * h

    def forward(p, step, h):
        for way in ways(h):
            block_out(p, step, h, way, mine(p, 2)).start()
        if h == 0:
            block_kept(p, step).start()

    with jax.named_scope("send_tokens"):
        for step in RING:
            for p in range(3):
                tables_out(p, step, mine(p, 0)).start()
                tokens_out(p, step, mine(p, 0)).start()
        for p in range(3):
            gathered[p][mine(p, 0)] = tok[:, STARTS[p]:STARTS[p] + WIDTHS[p]]
            notes[p, mine(p, 0)] = meta[p, mine(p, 0)]

    with jax.named_scope("pick_rows"):
        for p in range(3):
            for step in RING:
                tables_out(p, step, spot(p, 0, step)).wait_recv()
                tokens_out(p, step, spot(p, 0, step)).wait_recv()
            largest = jnp.maximum(jnp.maximum(notes[p, 0], notes[p, 1]), jnp.maximum(notes[p, 2], notes[p, 3]))
            total = notes[p, 0] + notes[p, 1] + notes[p, 2] + notes[p, 3]
            table = jnp.where(lax.broadcasted_iota(jnp.int32, (8, LANES), 0) < SIDE, largest, total)
            mixed[p] = table
            turned = table.T
            place = lax.broadcasted_iota(jnp.int32, (SLOTS, SIDE * 128), 1).astype(F32)
            for there in range(SIDE):
                full[:SLOTS, there * 512:(there + 1) * 512] = (turned[:SLOTS, there:there + 1] == place).astype(BF16)
            for step in RING + (0,):
                there = spot(p, 1, step)
                picks = pl.ds(pl.multiple_of(there * 512, 512), 512)

                @pl.loop(0, WIDTHS[p] // TILES[p])
                def _(n):
                    rows = gathered[p][:, :, tile(p, n)].reshape(SIDE * 128, TILES[p])
                    found = jnp.dot(full[:SLOTS, picks], rows, preferred_element_type=F32)
                    for d in range(SIDE * CORES):
                        cut[p][there, d // SIDE, d % SIDE, :, tile(p, n)] = found[d * BLOCK:(d + 1) * BLOCK].astype(BF16)

                if step:
                    picked_out(p, step, 0, mine(p, 1)).start()
                else:
                    forward(p, 0, 0)
    with jax.named_scope("second_half"):
        for step in RING:
            for p in range(3):
                picked_out(p, step, 1, mine(p, 1)).start()
        for p in range(3):
            forward(p, 0, 1)

    with jax.named_scope("relay_rows"):
        for h in range(CORES):
            for step in (3, 1, 2):
                for p in range(3):
                    picked_out(p, step, h, spot(p, 1, step)).wait_recv()
                    forward(p, step, h)

    def arrive(h):
        for p in range(3):
            for step in range(SIDE):
                for way in ways(h):
                    block_out(p, step, h, way, spot(p, 2, way)).wait_recv()
                if h == 0:
                    block_kept(p, step).wait()

    def line_up(h):
        for p in range(3):
            @pl.loop(0, WIDTHS[p] // TILES[p])
            def _(n):
                rows = held[p][h, :, :, :, tile(p, n)].astype(F32).reshape(HALF, TILES[p]).astype(BF16)
                if p != 1:
                    rows = jnp.dot(turns[p // 2], rows, preferred_element_type=F32).astype(BF16)
                full[:, tile(p, n, STARTS[p])] = rows

    def hide():
        @pl.loop(0, 4)
        def _(n):
            columns = pl.ds(pl.multiple_of(n * 256, 128), 256)
            gate = jnp.dot(full[...], gate_w[:, columns], preferred_element_type=F32)
            lin = jnp.dot(full[...], up_w[:, columns], preferred_element_type=F32)
            hid[:, columns] = (gate * (1.0 / (1.0 + jnp.exp(-gate))) * lin).astype(BF16)

    def answer(h, p):
        rows = hid if p == 1 else hid_t
        if p != 1:
            @pl.loop(0, 4)
            def _(n):
                columns = pl.ds(pl.multiple_of(n * 256, 128), 256)
                hid_t[:, columns] = jnp.dot(turns[1 - p // 2], hid[:, columns], preferred_element_type=F32).astype(BF16)

        @pl.loop(0, WIDTHS[p] // TILES[p])
        def _(n):
            result = jnp.dot(rows[...], down_w[:, tile(p, n, STARTS[p])], preferred_element_type=F32)
            for b in range(SIDE * SIDE):
                block = result[b * BLOCK:(b + 1) * BLOCK].astype(BF16)
                held[p][h, b // SIDE, b % SIDE, :, tile(p, n)] = block

        for step in RING + (0,):
            for way in ways(h):
                result_out(p, step, h, way, mine(p, 2)).start()
            if h == 0:
                result_kept(p, step).start()

    def landing(p, step, h):
        for way in ways(h):
            result_out(p, step, h, way, spot(p, 2, way)).wait_recv()
        if h == 0:
            result_kept(p, step).wait()

    with jax.named_scope("arrive_own"):
        arrive(0)
    with jax.named_scope("line_up"):
        loads[0].wait()
        line_up(0)
    with jax.named_scope("hidden"):
        loads[1].wait()
        loads[2].wait()
        hide()
    with jax.named_scope("answer"):
        loads[3].wait()
        for p in range(3):
            answer(0, p)
    with jax.named_scope("arrive_other"):
        arrive(1)
    with jax.named_scope("line_up"):
        line_up(1)
    with jax.named_scope("hidden"):
        hide()
    with jax.named_scope("relay_results_own"):
        for step in RING:
            for p in range(3):
                landing(p, step, 0)
                result_on(p, step, 0, mine(p, 1)).start()
    with jax.named_scope("answer"):
        for p in range(3):
            answer(1, p)
    with jax.named_scope("wait_sent"):
        for p in range(3):
            for step in RING:
                tables_out(p, step, mine(p, 0)).wait_send()
                tokens_out(p, step, mine(p, 0)).wait_send()
                for h in range(CORES):
                    picked_out(p, step, h, mine(p, 1)).wait_send()
            for step in range(SIDE):
                for h in range(CORES):
                    for way in ways(h):
                        block_out(p, step, h, way, mine(p, 2)).wait_send()
    with jax.named_scope("fetch_own"):
        for p in range(3):
            landing(p, 0, 0)
            fetched(p, 0, 0).start()
        for step in (3, 1, 2):
            for p in range(3):
                result_on(p, step, 0, spot(p, 1, step)).wait_recv()
                fetched(p, step, 0).start()
    with jax.named_scope("relay_results_other"):
        for step in RING:
            for p in range(3):
                landing(p, step, 1)
                result_on(p, step, 1, mine(p, 1)).start()
        for p in range(3):
            landing(p, 0, 1)
            fetched(p, 0, 1).start()

    with jax.named_scope("weighted_sum"):
        for p in range(3):
            token = lax.broadcasted_iota(jnp.int32, (SIDE * 128, SLOTS), 0).astype(F32)
            for there in range(SIDE):
                index = mixed[p, there:there + 1, :SLOTS]
                weight = mixed[p, SIDE + there:SIDE + there + 1, :SLOTS]
                full[:SIDE * 128, there * LANES:there * LANES + SLOTS] = jnp.where(token == index, weight, 0.0).astype(BF16)
            for step in (3, 1, 2):
                result_on(p, step, 1, spot(p, 1, step)).wait_recv()
                fetched(p, step, 1).start()
            for step in range(SIDE):
                for h in range(CORES):
                    fetched(p, step, h).wait()

            @pl.loop(0, WIDTHS[p] // TILES[p])
            def _(n):
                total = jnp.zeros((SIDE * 128, TILES[p]), F32)
                for there in range(SIDE):
                    rows = cut[p][there, :, :, :, tile(p, n)].astype(F32).reshape(SLOTS, TILES[p]).astype(BF16)
                    spread = full[:SIDE * 128, there * LANES:there * LANES + SLOTS]
                    total = total + jnp.dot(spread, rows, preferred_element_type=F32)
                for k in range(SIDE):
                    gathered[p][k, :, tile(p, n)] = total[k * 128:(k + 1) * 128].astype(BF16)

            for step in RING:
                sum_out(p, step, mine(p, 0)).start()
    with jax.named_scope("last_sum"):
        for p in range(3):
            total = gathered[p][mine(p, 0)].astype(F32)
            for step in RING:
                sum_out(p, step, spot(p, 0, step)).wait_recv()
                total = total + others[p][spot(p, 0, step)].astype(F32)
            out[:, STARTS[p]:STARTS[p] + WIDTHS[p]] = total.astype(BF16)
    for p in range(3):
        for step in RING:
            sum_out(p, step, mine(p, 0)).wait_send()
            for h in range(CORES):
                result_on(p, step, h, mine(p, 1)).wait_send()
        for step in range(SIDE):
            for h in range(CORES):
                for way in ways(h):
                    result_out(p, step, h, way, mine(p, 2)).wait_send()


ANY = pl.BlockSpec(memory_space=pl.ANY)
VMEM = pl.BlockSpec(memory_space=pltpu.VMEM)
DMA = pltpu.SemaphoreType.DMA


def blocks(leading):
    return [jax.ShapeDtypeStruct(leading + (w,), BF16) for w in WIDTHS]


def scratch(leading):
    return [pltpu.VMEM(leading + (w,), BF16) for w in WIDTHS]


def turn_matrices():
    row = jnp.arange(HALF, dtype=jnp.int32)
    k, i, j, s = row // 160, row // 40 % 4, row // 10 % 4, row % 10
    there = (i * 160 + j * 40 + k * 10 + s)[:, None] == row[None, :]
    return jnp.stack([there, there.T]).astype(BF16)


def tables(expert_ids, gate_weights):
    rows = expert_ids.shape[0]
    experts = SIDE ** 3 * CORES
    hit = expert_ids[:, :, None] == jnp.arange(experts, dtype=jnp.int32)[None, None, :]
    named = jnp.any(hit, axis=1)
    weight = jnp.sum(jnp.where(hit, gate_weights[:, :, None], 0.0), axis=1)
    below = (jnp.arange(rows)[:, None] > jnp.arange(rows)[None, :]).astype(BF16)
    place = jnp.dot(below, named.astype(BF16), preferred_element_type=F32).astype(jnp.int32)
    place = jnp.where(named, place, -1)
    pick = place.T[:, None, :] == jnp.arange(CAP, dtype=jnp.int32)[None, :, None]
    token = jnp.max(jnp.where(pick, jnp.arange(rows, dtype=jnp.int32).astype(F32)[None, None, :], -1.0), axis=2)
    amount = jnp.sum(jnp.where(pick, weight.T[:, None, :], 0.0), axis=2)
    shape = (SIDE, SIDE, SIDE, CORES, CAP)
    token, amount = token.reshape(shape), amount.reshape(shape)
    pos, core = whereabouts()
    token = jnp.where(core == 0, token, token[:, :, :, ::-1])
    amount = jnp.where(core == 0, amount, amount[:, :, :, ::-1])
    made = []
    for a1, a2, a3 in ORDERS:
        mine = (jnp.arange(SIDE) == pos[a1])[None, None, None, None, :, None]
        order = (a1, a2, 3, a3, 4)
        index = token.transpose(order)[:, :, :, :, None, :]
        index = jnp.where(mine & (index >= 0), index + (128 * pos[a1]).astype(F32), -1.0)
        value = jnp.where(mine, amount.transpose(order)[:, :, :, :, None, :], 0.0)
        index = jnp.pad(index.reshape(SIDE, SIDE, SLOTS), ((0, 0), (0, 0), (0, LANES - SLOTS)), constant_values=-1.0)
        value = jnp.pad(value.reshape(SIDE, SIDE, SLOTS), ((0, 0), (0, 0), (0, LANES - SLOTS)))
        made.append(jnp.concatenate([index, value], axis=1))
    return jnp.stack(made)


def body(tokens, expert_ids, gate_weights, w_gate, w_up, w_down):
    meta = tables(expert_ids, gate_weights)
    split = (SIDE, CORES, SIDE, BLOCK)
    out, *_ = pl.pallas_call(
        layer_kernel,
        out_shape=[jax.ShapeDtypeStruct(tokens.shape, BF16)] + blocks(split) * 3,
        in_specs=[VMEM, VMEM] + [ANY] * 4,
        out_specs=[VMEM] + [ANY] * 9,
        scratch_shapes=scratch((SIDE, 128)) + scratch(split) + scratch((CORES, SIDE, SIDE, BLOCK)) + scratch((SIDE, 128)) + [
            pltpu.VMEM(w_gate.shape[1:], BF16), pltpu.VMEM(w_up.shape[1:], BF16), pltpu.VMEM(w_down.shape[1:], BF16),
            pltpu.VMEM((2, HALF, HALF), BF16),
            pltpu.VMEM((HALF, tokens.shape[1]), BF16),
            pltpu.VMEM((HALF, w_gate.shape[2]), BF16),
            pltpu.VMEM((HALF, w_gate.shape[2]), BF16),
            pltpu.VMEM((3, SIDE, 8, LANES), F32),
            pltpu.VMEM((3, 8, LANES), F32),
        ] + [
            DMA((4,)), DMA((3, SIDE)), DMA((3, SIDE)), DMA((3, SIDE)), DMA((3, SIDE)),
            DMA((3, SIDE, CORES)), DMA((3, SIDE, CORES)), DMA((3, SIDE, CORES, SIDE)), DMA((3, SIDE, CORES, SIDE)),
            DMA((3, SIDE)), DMA((3, SIDE, CORES, SIDE)), DMA((3, SIDE, CORES, SIDE)), DMA((3, SIDE)),
            DMA((3, SIDE, CORES)), DMA((3, SIDE, CORES)), DMA((3, SIDE, CORES)), DMA((3, SIDE)), DMA((3, SIDE)),
        ],
        compiler_params=pltpu.CompilerParams(
            collective_id=0, has_side_effects=True, vmem_limit_bytes=62 * 2 ** 20
        ),
        name="layer",
    )(tokens, meta, w_gate[0], w_up[0], w_down[0], turn_matrices())
    return out


def solution(mesh):
    spec = P(("group", "local"), None)
    wide = P(("group", "local"), None, None)
    return jax.shard_map(
        body, mesh=mesh, in_specs=(spec, spec, spec, wide, wide, wide), out_specs=spec, check_vma=False
    )
```

time: 410 us -> 228 us (0.56)
  Pallas kernels: 0 us -> 212 us
  blocking collectives: 114 us -> 0 us
  waiting for transfers between devices: 113 us -> 0 us
  local copies, waits for them, and re-layouts: 93.9 us -> 8.01 us
  matrix products: 58.4 us -> 0.19 us
  other arithmetic: 20.1 us -> 4.07 us
  starting transfers between devices: 8.84 us -> 0 us
    pallas_call x0 -> x1, Pallas kernels: none -> 212 us  [body(): pl.pallas_call(layer_kernel, out_shape=[jax.ShapeDtypeStruct(tokens.shape...]
    all_to_all x1 -> x0, blocking collectives: 114 us -> none  [body(): lax.all_to_all(jnp.concatenate(parts, axis=1), ('group', 'local'), split_...]
    all_to_all x1 -> x0, waiting for transfers between devices: 113 us -> none  [body(): lax.all_to_all(results, ('group', 'local'), split_axis=0, concat_axis=0,...]
    dot_general x15 -> x1, matrix products: 58.4 us -> 0.19 us  [tables(): jnp.dot(below, named.astype(BF16), preferred_element_type=F32)]
    reshape x12 -> x0, local copies, waits for them, and re-layouts: 55.2 us -> none  [the longest x4 19.9 us: body(): arrived[:, q * CAP:(q + 1) * CAP].reshape(experts * CAP, quarter)]
    slice x2 -> x0, local copies, waits for them, and re-layouts: 19.2 us -> none  [the longest x1 11.9 us: body(): back = returned[:, q * CAP:(q + 1) * CAP].reshape(experts * CAP, quarter)]
    concatenate x3 -> x0, other arithmetic: 18.1 us -> none  [the longest x1 12.8 us: body(): jnp.concatenate([jnp.dot(hidden, w_down[0][:, q * quarter:(q + 1) * quart...]
    concatenate x2 -> x0, local copies, waits for them, and re-layouts: 12.8 us -> none  [the longest x1 12.4 us: body(): jnp.concatenate(parts, axis=1)]
  transfers between devices with their start and end apart: 1 -> 0, of which waited for: 1 -> 0; matrix products, arithmetic and copies ran while one was open for 1% -> 0% of each run, Pallas kernels for 0% -> 0%
where the time goes in v2:
time: 228 us; the launch traced here: 225 us
  Pallas kernels  212 us (93%)
  local copies, waits for them, and re-layouts  8.01 us (4%)
  other arithmetic  4.07 us (2%)
    pallas_call x1, Pallas kernels, body(): pl.pallas_call(layer_kernel, out_shape=[jax.ShapeDtypeStruct(tokens.shape...  212 us

profile of v2, /device:TPU:26, one launch (start us, length us, event | category | flops | bytes accessed | tf_op | source)
XLA Modules:
  0.0 224.8 jit_solution(8895301025027893126)
XLA Ops:
  0.3 0.1 and.154
  0.5 0.1 and.146
  0.6 0.8 copy.26
  1.4 0.3 fusion.1
  1.8 0.2 fusion
  2.0 0.8 copy.31
  2.8 0.3 select_reduce_fusion.2
  3.2 0.4 select_reduce_fusion.1
  3.8 0.2 rev.6
  4.1 0.2 and.150
  4.4 0.1 rev.7
  4.9 0.2 and.164
  5.2 0.2 and.157
  5.6 0.3 broadcast_in_dim.146
  5.9 0.3 broadcast_in_dim.150
  6.3 0.3 broadcast_in_dim.136
  6.6 0.3 broadcast_in_dim.152
  7.0 0.3 broadcast_in_dim.148
  7.4 0.3 broadcast_in_dim.143
  7.7 0.7 pad_maximum_fusion.meta
  8.4 0.6 iota_compare_fusion.1
  8.9 1.5 add_convert_fusion.turn
  10.4 212.2 %layer.1 = (bf16[128,3584]{1,0:T(8,128)(2,1)}, bf16[4,2,4,40,1152]{4,3,2,1,0:T(8,128)(2,1)}, bf16[4,2,4,40,1280]{4,3,2,1,0:T(8,128)(2,1)}, bf16[4,2,4,40,1152]{4...) custom-call(bf16[128,3584]{1,0:T(8,128)(2,1)} %tok.1, ...), custom_call_target="tpu_custom_call" | custom-call | tf_op jit(solution)/shard_map/layer/pallas_call | solution.py:407
  222.6 2.2 copy.43
  (40 shorter events, 1.9 us)
